TPU v7x, 256 devices: a whole 4x4x8 slice. The times are simulated.
256 devices in a mesh: grp: 8 (over z_lo, y), seq: 4 (over z_hi), smp: 8 (over x, core).
Axes of the slice: x: 4, y: 4, z: 8 (z_hi: 4, z_lo: 2; z = z_hi * 2 + z_lo), core: 2. Of those that a mesh axis runs over, the one named last changes fastest.
Arguments:
- prompt_x: bfloat16 [16384, 5120], P(('grp', 'seq')), parts along dimension 0, may hold values from -6 to 6
- sampled_x: bfloat16 [128, 4, 5120], P('grp'), parts along dimension 0, may hold values from -6 to 6
- w_query: bfloat16 [5120, 8192], P('seq', 'smp'), may hold values from -0.078125 to 0.078125
- w_key: bfloat16 [5120, 1024], P('seq', 'smp'), may hold values from -0.078125 to 0.078125
- w_value: bfloat16 [5120, 1024], P('seq', 'smp'), may hold values from -0.078125 to 0.078125
- q_gain: float32 [128], replicated, may hold values from 0.25 to 1.75
- k_gain: float32 [128], replicated, may hold values from 0.25 to 1.75
Outputs:
- prefill_out: bfloat16 [16384, 8192], P(('grp', 'seq'), 'smp'), parts along dimension 0
- decode_out: bfloat16 [128, 4, 8192], P(('grp', 'smp')), parts along dimension 0
There are 8 independent parts, one for each index of `grp`. A program takes and returns all parts, laid end to end along the dimension named above; an argument that names none is the same for every part. Nothing has to cross between parts.
All inputs are finite; a program needn't handle non-finite values.
Results may differ from a plain program's by a relative error of at most 0.023.
Values may be sent and summed in bfloat16 or wider, within the bound.
A program may use at most 128 MiB of HBM per device.

v0:
```python
import jax
import jax.numpy as jnp
from jax import lax
from jax.sharding import PartitionSpec as P

HD = 128


neg_fill = -1e30


def rope_parts(positions):
    half = HD // 2
    freq = 1000000.0 ** (-(jnp.arange(half, dtype=jnp.float32) * 2.0 / HD))
    angle = positions.astype(jnp.float32)[:, None] * freq[None, :]
    return (jnp.cos(angle), jnp.sin(angle))


def norm_rotate(values, gain, positions):
    scaled = values * lax.rsqrt(jnp.mean(values * values, -1, keepdims=True) + 1e-06) * gain
    cosine, sine = rope_parts(positions)
    cosine = cosine[:, None, :]
    sine = sine[:, None, :]
    first = scaled[..., : HD // 2]
    second = scaled[..., HD // 2 :]
    return jnp.concatenate([first * cosine - second * sine, second * cosine + first * sine], -1)


def prompt_partial(query, keys, values, form, scale):
    key_dims = form.replace("m", "").replace("k", "").replace("d", "")
    scores = (
        jnp.einsum(
            "jmkgd," + form + "->jmkg" + key_dims, query, keys, preferred_element_type=jnp.float32
        )
        * scale
    )
    shape = scores.shape
    flat = scores.reshape(shape[:4] + (-1,))
    top = flat.max(-1)
    prob = jnp.exp(flat - top[..., None])
    total = prob.sum(-1)
    weights = prob.astype(jnp.bfloat16).reshape(shape)
    acc = jnp.einsum(
        "jmkg" + key_dims + "," + form + "->jmkgd",
        weights,
        values,
        preferred_element_type=jnp.float32,
    )
    return (top, total, acc)


def finish_own(top, total, acc, own_q, own_k, own_v, steps, scale):
    own_scores = (
        jnp.einsum("itmkgd,iumkd->itmkgu", own_q, own_k, preferred_element_type=jnp.float32) * scale
    )
    allowed = jnp.arange(steps)[None, :] <= jnp.arange(steps)[:, None]
    mask_six = allowed[None, :, None, None, None, :]
    own_scores = jnp.where(mask_six, own_scores, neg_fill)
    final_top = jnp.maximum(top, own_scores.max(-1))
    own_prob = jnp.where(mask_six, jnp.exp(own_scores - final_top[..., None]), 0.0)
    factor = jnp.exp(top - final_top)
    total = total * factor + own_prob.sum(-1)
    acc = acc * factor[..., None] + jnp.einsum(
        "itmkgu,iumkd->itmkgd",
        own_prob.astype(jnp.bfloat16),
        own_v,
        preferred_element_type=jnp.float32,
    )
    return acc / total[..., None]


def local(prompt_x, sampled_x, w_query, w_key, w_value, q_gain, k_gain):
    n_seq = lax.axis_size("seq")
    n_smp = lax.axis_size("smp")
    seq_index = lax.axis_index("seq")
    rows = prompt_x.shape[0]
    samples, steps, width = sampled_x.shape
    length = rows * n_seq
    q_cols = w_query.shape[1]
    kv_cols = w_key.shape[1]
    local_q = q_cols // HD
    local_kv = kv_cols // HD
    group = local_q // local_kv
    scale = HD ** (-0.5)
    inputs = jnp.concatenate([prompt_x, sampled_x.reshape(samples * steps, width)], 0)
    count = inputs.shape[0]
    pieces = (
        lax.all_gather(w_query, "seq", axis=0, tiled=True),
        lax.all_gather(w_key, "seq", axis=0, tiled=True),
        lax.all_gather(w_value, "seq", axis=0, tiled=True),
    )
    query_all, key_all, value_all = tuple(
        (jnp.dot(inputs, piece, preferred_element_type=jnp.float32) for piece in pieces)
    )
    positions = jnp.concatenate(
        [
            seq_index * rows + jnp.arange(rows, dtype=jnp.int32),
            jnp.tile(length + jnp.arange(steps, dtype=jnp.int32), samples),
        ]
    )
    query = norm_rotate(query_all.reshape(count, local_q, HD), q_gain, positions).astype(
        jnp.bfloat16
    )
    key = norm_rotate(key_all.reshape(count, local_kv, HD), k_gain, positions).astype(jnp.bfloat16)
    value = value_all.astype(jnp.bfloat16)
    prompt_query = query[:rows]
    prompt_key = key[:rows].reshape(rows, kv_cols)
    prompt_value = value[:rows]
    moved = lax.all_to_all(
        prompt_query.reshape(rows, q_cols), "seq", split_axis=1, concat_axis=0, tiled=True
    )
    per_dev = local_q // n_seq
    heads_q = moved.reshape(length, per_dev, HD)
    full_key, full_value = (
        lax.all_gather(prompt_key, "seq", axis=0, tiled=True),
        lax.all_gather(prompt_value, "seq", axis=0, tiled=True),
    )
    key_one = full_key.reshape(length, local_kv, HD)[:, 0]
    value_one = full_value.reshape(length, local_kv, HD)[:, 0]
    block = min(512, length)

    def one_block(index):
        start = index * block
        rows_q = lax.dynamic_slice_in_dim(heads_q, start, block, 0)
        scores = (
            jnp.einsum("bhd,ld->hbl", rows_q, key_one, preferred_element_type=jnp.float32) * scale
        )
        allowed = (
            jnp.arange(length, dtype=jnp.int32)[None, :]
            <= (start + jnp.arange(block, dtype=jnp.int32))[:, None]
        )
        scores = jnp.where(allowed, scores, neg_fill)
        top = scores.max(-1, keepdims=True)
        prob = jnp.where(allowed, jnp.exp(scores - top), 0.0)
        total = prob.sum(-1)
        out = (
            jnp.einsum(
                "hbl,ld->bhd",
                prob.astype(jnp.bfloat16),
                value_one,
                preferred_element_type=jnp.float32,
            )
            / total.T[..., None]
        )
        return out.astype(jnp.bfloat16)

    attended = lax.map(one_block, jnp.arange(length // block, dtype=jnp.int32)).reshape(
        length, per_dev * HD
    )
    prefill = lax.all_to_all(attended, "seq", split_axis=0, concat_axis=1, tiled=True)
    dec_query = query[rows:].reshape(samples * steps, q_cols)
    dec_key = key[rows:].reshape(samples * steps, kv_cols)
    dec_value = value[rows:]
    own_count = samples // n_smp
    jrows = own_count * steps
    mine_q, mine_k, mine_v = (
        lax.all_to_all(dec_query, "smp", split_axis=0, concat_axis=1, tiled=True),
        lax.all_to_all(dec_key, "smp", split_axis=0, concat_axis=1, tiled=True),
        lax.all_to_all(dec_value, "smp", split_axis=0, concat_axis=1, tiled=True),
    )
    query_five = mine_q.reshape(jrows, n_smp, local_kv, group, HD)
    cache_key, cache_value = (
        lax.all_gather(prompt_key.reshape(1, rows, kv_cols), ("seq", "smp"), axis=0, tiled=True),
        lax.all_gather(prompt_value.reshape(1, rows, kv_cols), ("seq", "smp"), axis=0, tiled=True),
    )
    cache_key = cache_key.reshape(n_seq, n_smp, rows, local_kv, HD)
    cache_value = cache_value.reshape(n_seq, n_smp, rows, local_kv, HD)
    top, total, acc = prompt_partial(query_five, cache_key, cache_value, "smrkd", scale)
    shaped = (own_count, steps, n_smp, local_kv, group)
    finished = finish_own(
        top.reshape(shaped),
        total.reshape(shaped),
        acc.reshape(shaped + (HD,)),
        mine_q.reshape(own_count, steps, n_smp, local_kv, group, HD),
        mine_k.reshape(own_count, steps, n_smp, local_kv, HD),
        mine_v.reshape(own_count, steps, n_smp, local_kv, HD),
        steps,
        scale,
    )
    decode = finished.reshape(own_count, steps, n_smp * q_cols).astype(jnp.bfloat16)
    return (prefill, decode)


def solution(mesh):
    in_specs = (
        P(("grp", "seq"), None),
        P("grp", None, None),
        P("seq", "smp"),
        P("seq", "smp"),
        P("seq", "smp"),
        P(),
        P(),
    )
    out_specs = (P(("grp", "seq"), "smp"), P(("grp", "smp"), None, None))
    return jax.shard_map(local, mesh=mesh, in_specs=in_specs, out_specs=out_specs, check_vma=False)
```

profile of v0, /device:TPU:1, one launch (start us, length us, event | category | flops | bytes accessed | tf_op | source)
XLA Modules:
  0.0 487.1 jit_solution(9113979558395184461)
XLA Ops:
  7.2 0.7 all-gather.11.cloned.1.call-update
  7.9 0.7 all-gather.13.cloned.1.call-update
  8.7 0.7 all-gather.9.cloned.1.call-update
  9.4 1.5 reshape.394
  11.1 5.2 %constant_dynamic-update-slice_fusion.2 = bf16[576,5120]{1,0:T(8,128)(2,1)} fusion(bf16[512,5120]{1,0:T(8,128)(2,1)} %param.9), kind=kLoop, calls=%fused_computation.94 | loop fusion | bytes 10485760
  16.3 0.9 constant_dynamic-update-slice_fusion.1
  17.2 35.0 %all-gather.11.cloned.1.call-done = bf16[5120,128]{1,0:T(8,128)(2,1)} async-done(((bf16[1280,128]{1,0:T(8,128)(2,1)}), bf16[5120,128]{1,0:T(8,128)(2,1)}) %all-gather.11.cloned.1.call-update) | async-done | bytes 1310736 | tf_op jit(solution)/shard_map/all_gather | solution.py:89
  52.3 4.8 multiply_reduce_fusion.1
  57.4 0.7 fusion.61
  58.0 0.7 fusion.62
  58.7 0.6 multiply_cosine_fusion.1
  59.4 0.7 copy.158
  60.1 5.2 %all-to-all-start.3 = ((bf16[8,8,128]{2,1,0:T(8,128)(2,1)}), bf16[8,8,128]{2,1,0:T(8,128)(2,1)S(1)}, u32[]{:S(2)}, u32[]{:S(2)}) async-start(bf16[8,8,128]{2,1,0:T(8,128)(2,1)} %bitcast.29), calls=%async_computation.3 | async-start | bytes 32768 | tf_op jit(solution)/shard_map/all_to_all | solution.py:158
  65.3 25.8 %all-gather.13.cloned.1.call-done = bf16[5120,128]{1,0:T(8,128)(2,1)} async-done(((bf16[1280,128]{1,0:T(8,128)(2,1)}), bf16[5120,128]{1,0:T(8,128)(2,1)}) %all-gather.13.cloned.1.call-update) | async-done | bytes 1310736 | tf_op jit(solution)/shard_map/all_gather | solution.py:90
  91.0 4.7 convolution_convert_fusion
  95.8 0.6 slice_bitcast_fusion
  96.4 183.3 %all-gather.9.cloned.1.call-done = bf16[5120,1024]{1,0:T(8,128)(2,1)} async-done(((bf16[1280,1024]{1,0:T(8,128)(2,1)}), bf16[5120,1024]{1,0:T(8,128)(2,1)}) %all-gather.9.cloned.1.call-update) | async-done | bytes 10485776 | tf_op jit(solution)/shard_map/all_gather | solution.py:88
  279.7 10.7 %convolution_bitcast_fusion = f32[72,8,8,128]{3,1,2,0:T(8,128)S(1)} fusion(bf16[576,5120]{1,0:T(8,128)(2,1)} %constant_dynamic-update-slice_fusion.1, bf16[5120,1024]{1,0:T(8,128)(2,1)} %all-gather.9.cloned.1.call-done), kind=kOutput, calls=%fused_computation.42 | convolution fusion | flops 6039797760 | bytes 18743296 | tf_op jit(solution)/shard_map/dot_general | solution.py:93
  290.4 0.5 copy.193
  290.9 2.2 copy.147
  293.2 0.7 multiply_reduce_fusion
  294.0 2.1 multiply_multiply_fusion
  296.5 5.7 %all-to-all-start.4 = ((bf16[8,8,128]{2,1,0:T(8,128)(2,1)}), bf16[8,8,128]{2,1,0:T(8,128)(2,1)S(1)}, u32[]{:S(2)}, u32[]{:S(2)}) async-start(bf16[8,8,128]{2,1,0:T(8,128)(2,1)} %slice_bitcast_fusion), calls=%async_computation.4 | async-start | bytes 32768 | tf_op jit(solution)/shard_map/all_to_all | solution.py:159
  302.4 0.7 all_to_all.69
  303.2 3.8 all-to-all-done.4
  306.9 4.0 all-to-all-start.2
  310.9 1.1 fusion.53
  312.0 4.2 all-to-all-done.2
  316.2 5.4 %all-to-all-start = ((bf16[512,4,256]{0,2,1:T(8,128)(2,1)}), bf16[512,4,256]{0,2,1:T(8,128)(2,1)S(1)}, u32[]{:S(2)}, u32[]{:S(2)}) async-start(bf16[512,4,256]{0,2,1:T(8,128)(2,1)} %bitcast.7), calls=%async_computation | async-start | bytes 2097152 | tf_op jit(solution)/shard_map/all_to_all | solution.py:109
  321.6 0.7 slice.48
  322.2 51.1 %all-gather = bf16[2048,1,128]{0,2,1:T(8,128)(2,1)S(1)} all-gather(bf16[512,1,128]{0,2,1:T(8,128)(2,1)S(1)} %copy-done), channel_id=2, replica_groups=mesh['grp'=8,'seq'=4,'smp'=8] {'seq'}, dimensions={0}, use_global_device_ids=true | all-gather | bytes 655360 | tf_op jit(solution)/shard_map/all_gather | solution.py:115
  373.7 15.4 %all_gather.25 = bf16[2048,128]{1,0:T(8,128)(2,1)S(1)} all-gather(bf16[512,128]{1,0:T(8,128)(2,1)} %slice.48), channel_id=1, replica_groups=mesh['grp'=8,'seq'=4,'smp'=8] {'seq'}, dimensions={0}, use_global_device_ids=true | all-gather | bytes 655360 | tf_op jit(solution)/shard_map/all_gather | solution.py:116
  389.1 3.9 copy.194
  393.1 7.1 %bitcast_reduce_fusion.1 = (f32[8,8,8]{2,0,1:T(8,128)S(1)}, f32[8,4,512,8,8]{2,4,3,1,0:T(8,128)}) fusion(bf16[8,8,8,128]{3,1,2,0:T(8,128)(2,1)S(1)} %bitcast.177, bf16[4,8,512,128,1]{2,1,0,3,4:T(8,128)(2,1)S(1)} %bitcast.169), kind=kOutput, calls=%fused_computation.30 | convolution fusion | flops 270532096 | bytes 8521728 | tf_op jit(solution)/shard_map/jmkgd,smrkd->jmkgsr/dot_general | solution.py:32
  400.2 1.4 fusion.85
  401.5 0.5 copy.148
  402.9 51.7 %while.10 = (s32[]{:T(128)}, bf16[4,512,2,128]{1,3,2,0:T(8,128)(2,1)}, s32[4]{0:T(128)}, bf16[2048,2,128]{2,1,0:T(2,128)(2,1)S(1)}, bf16[2048,128]{1,0:T(8,128)(...) while((s32[]{:T(128)}, ...), condition=%wide.region_5.6_spmd, body=%wide.region_2.5_spmd.sunk | while | flops 1087638016 | bytes 13644455 | solution.py:147
  402.9 1.2 dynamic_slice.11
  404.8 0.7 iota_compare_fusion.3
  405.5 6.0 %fusion.103 = (f32[2,512]{1,0:T(2,128)}, bf16[2,512,2048]{2,1,0:T(8,128)(2,1)}) fusion(pred[512,2048]{1,0:T(8,128)(4,1)S(1)} %iota_compare_fusion.3, bf16[2048,128]{1,0:T(8,128)(2,1)S(1)} %get-tuple-element.188, bf16[512,2,128]{2,1,0:T(2,128)(2,1)S(1)} %constant_dynamic-slice_fusion.2), kind=kOutput, calls=%fused_computation.103.clone.1 | convolution fusion | flops 549455872 | bytes 6033408 | tf_op jit(solution)/shard_map/while/body/eval_jaxpr/sub | solution.py:134
  411.5 3.4 fusion.104
  415.1 0.7 constant_dynamic-update-slice_fusion.4
  415.8 1.2 dynamic_slice.11
  417.7 0.7 iota_compare_fusion.3
  418.4 6.0 %fusion.103 = (f32[2,512]{1,0:T(2,128)}, bf16[2,512,2048]{2,1,0:T(8,128)(2,1)}) fusion(pred[512,2048]{1,0:T(8,128)(4,1)S(1)} %iota_compare_fusion.3, bf16[2048,128]{1,0:T(8,128)(2,1)S(1)} %get-tuple-element.188, bf16[512,2,128]{2,1,0:T(2,128)(2,1)S(1)} %constant_dynamic-slice_fusion.2), kind=kOutput, calls=%fused_computation.103.clone.1 | convolution fusion | flops 549455872 | bytes 6033408 | tf_op jit(solution)/shard_map/while/body/eval_jaxpr/sub | solution.py:134
  424.4 3.5 fusion.104
  428.0 0.7 constant_dynamic-update-slice_fusion.4
  428.8 1.2 dynamic_slice.11
  430.7 0.7 iota_compare_fusion.3
  431.4 6.0 %fusion.103 = (f32[2,512]{1,0:T(2,128)}, bf16[2,512,2048]{2,1,0:T(8,128)(2,1)}) fusion(pred[512,2048]{1,0:T(8,128)(4,1)S(1)} %iota_compare_fusion.3, bf16[2048,128]{1,0:T(8,128)(2,1)S(1)} %get-tuple-element.188, bf16[512,2,128]{2,1,0:T(2,128)(2,1)S(1)} %constant_dynamic-slice_fusion.2), kind=kOutput, calls=%fused_computation.103.clone.1 | convolution fusion | flops 549455872 | bytes 6033408 | tf_op jit(solution)/shard_map/while/body/eval_jaxpr/sub | solution.py:134
  437.3 3.4 fusion.104
  440.9 0.7 constant_dynamic-update-slice_fusion.4
  441.7 1.2 dynamic_slice.11
  443.6 0.7 iota_compare_fusion.3
  444.3 6.0 %fusion.103 = (f32[2,512]{1,0:T(2,128)}, bf16[2,512,2048]{2,1,0:T(8,128)(2,1)}) fusion(pred[512,2048]{1,0:T(8,128)(4,1)S(1)} %iota_compare_fusion.3, bf16[2048,128]{1,0:T(8,128)(2,1)S(1)} %get-tuple-element.188, bf16[512,2,128]{2,1,0:T(2,128)(2,1)S(1)} %constant_dynamic-slice_fusion.2), kind=kOutput, calls=%fused_computation.103.clone.1 | convolution fusion | flops 549455872 | bytes 6033408 | tf_op jit(solution)/shard_map/while/body/eval_jaxpr/sub | solution.py:134
  450.2 3.4 fusion.104
  453.8 0.7 constant_dynamic-update-slice_fusion.4
  454.6 4.6 all-to-all-start.1
  459.2 1.1 fusion.64
  460.3 3.1 fusion.44
  463.5 3.0 fusion.42
  466.9 0.7 convert_element_type.47
  467.6 11.7 %all-to-all-done.1 = bf16[4,512,256]{1,2,0:T(8,128)(2,1)S(1)} async-done(((bf16[4,512,256]{1,2,0:T(8,128)(2,1)}), bf16[4,512,256]{1,2,0:T(8,128)(2,1)S(1)}, u32[]{:S(2)}, u32[]{:S(2)}) %all-to-all-start.1) | async-done | bytes 1048608 | tf_op jit(solution)/shard_map/all_to_all | solution.py:150
  479.3 1.3 copy.171
  (63 shorter events, 4.3 us)
Async XLA Ops:
  7.2 45.1 %all-gather.11.cloned.1.call-start = ((), (), s32[]{:S(2)}) async-start(), calls=%async_computation.6 | async-start | bytes 1638400 | tf_op jit(solution)/shard_map/all_gather | solution.py:89
  7.9 83.1 %all-gather.13.cloned.1.call-start = ((), (), s32[]{:S(2)}) async-start(), calls=%async_computation.7 | async-start | bytes 1638400 | tf_op jit(solution)/shard_map/all_gather | solution.py:90
  8.6 271.0 %all-gather.9.cloned.1.call-start = ((), (), s32[]{:S(2)}) async-start(), calls=%async_computation.5 | async-start | bytes 13107200 | tf_op jit(solution)/shard_map/all_gather | solution.py:88
  9.4 379.7 %all-gather.17.cloned.1.call-start = ((), (), s32[]{:S(2)}) async-start(), calls=%async_computation.9 | async-start | bytes 4325376 | tf_op jit(solution)/shard_map/all_gather | solution.py:163
  17.2 40.0 %copy-start.5 = (f32[128]{0:T(128)S(1)}, f32[128]{0:T(128)}, u32[]{:S(2)}) copy-start(f32[128]{0:T(128)} %param.15) | copy-start | bytes 1540
  60.1 236.4 %all-to-all-start.3 = ((bf16[8,8,128]{2,1,0:T(8,128)(2,1)}), bf16[8,8,128]{2,1,0:T(8,128)(2,1)S(1)}, u32[]{:S(2)}, u32[]{:S(2)}) async-start(bf16[8,8,128]{2,1,0:T(8,128)(2,1)} %bitcast.29), calls=%async_computation.3 | async-start | bytes 32768 | tf_op jit(solution)/shard_map/all_to_all | solution.py:158
  290.9 3.1 copy-start.2
  296.5 25.8 %copy-start = (bf16[512,1,128]{0,2,1:T(8,128)(2,1)S(1)}, bf16[512,1,128]{0,2,1:T(8,128)(2,1)}, u32[]{:S(2)}) copy-start(bf16[512,1,128]{0,2,1:T(8,128)(2,1)} %fusion.62) | copy-start | bytes 393220
  296.5 10.4 %all-to-all-start.4 = ((bf16[8,8,128]{2,1,0:T(8,128)(2,1)}), bf16[8,8,128]{2,1,0:T(8,128)(2,1)S(1)}, u32[]{:S(2)}, u32[]{:S(2)}) async-start(bf16[8,8,128]{2,1,0:T(8,128)(2,1)} %slice_bitcast_fusion), calls=%async_computation.4 | async-start | bytes 32768 | tf_op jit(solution)/shard_map/all_to_all | solution.py:159
  306.9 9.3 %all-to-all-start.2 = ((bf16[8,8,1024]{2,1,0:T(8,128)(2,1)}), bf16[8,8,1024]{2,1,0:T(8,128)(2,1)S(1)}, u32[]{:S(2)}, u32[]{:S(2)}) async-start(bf16[8,8,1024]{2,1,0:T(8,128)(2,1)} %all_to_all.69), calls=%async_computation.2 | async-start | bytes 262144 | tf_op jit(solution)/shard_map/all_to_all | solution.py:157
  316.2 85.4 %all-to-all-start = ((bf16[512,4,256]{0,2,1:T(8,128)(2,1)}), bf16[512,4,256]{0,2,1:T(8,128)(2,1)S(1)}, u32[]{:S(2)}, u32[]{:S(2)}) async-start(bf16[512,4,256]{0,2,1:T(8,128)(2,1)} %bitcast.7), calls=%async_computation | async-start | bytes 2097152 | tf_op jit(solution)/shard_map/all_to_all | solution.py:109
  321.6 141.9 %all-gather.15.cloned.1.call-start = ((), (), s32[]{:S(2)}) async-start(), calls=%async_computation.8 | async-start | bytes 4325376 | tf_op jit(solution)/shard_map/all_gather | solution.py:164
  321.6 78.6 %copy-start.3 = (pred[4,4]{1,0:T(4,128)(4,1)}, pred[4,4]{1,0:T(4,128)(4,1)S(1)}, u32[]{:S(2)}) copy-start(pred[4,4]{1,0:T(4,128)(4,1)S(1)} %iota_compare_fusion.1) | copy-start | bytes 52
  454.6 24.7 %all-to-all-start.1 = ((bf16[4,512,256]{1,2,0:T(8,128)(2,1)}), bf16[4,512,256]{1,2,0:T(8,128)(2,1)S(1)}, u32[]{:S(2)}, u32[]{:S(2)}) async-start(bf16[4,512,256]{1,2,0:T(8,128)(2,1)} %bitcast.11), calls=%async_computation.1 | async-start | bytes 2097152 | tf_op jit(solution)/shard_map/all_to_all | solution.py:150
  463.4 3.0 copy-start.1
  463.4 3.0 copy-start.4
Sparse Core Ops, SparseCore 0:
  9.8 42.4 all-gather.10
  54.1 36.9 all-gather.12
  92.8 186.7 all-gather.8
  282.6 85.3 all-gather.16
  373.8 61.6 all-gather.14
where the time goes:
time: 492 us; the launch traced here: 487 us
  waiting for transfers between devices  266 us (54%)
  matrix products  69.7 us (14%)
  blocking collectives  66.5 us (14%)
  local copies, waits for them, and re-layouts  30.1 us (6%)
  starting transfers between devices  25 us (5%)
  between operations  14.1 us (3%)
  other arithmetic  13.3 us (3%)
    all_gather x1, waiting for transfers between devices, local(): lax.all_gather(w_query, 'seq', axis=0, tiled=True)  183 us
    all_gather x1, blocking collectives, local(): lax.all_gather(prompt_key, 'seq', axis=0, tiled=True)  51.1 us
    all_gather x1, waiting for transfers between devices, local(): lax.all_gather(w_key, 'seq', axis=0, tiled=True)  35 us
    all_gather x1, waiting for transfers between devices, local(): lax.all_gather(w_value, 'seq', axis=0, tiled=True)  25.8 us
    sub x4, matrix products, one_block(): prob = jnp.where(allowed, jnp.exp(scores - top), 0.0)  23.8 us
    dot_general x3, matrix products, local(): jnp.dot(inputs, piece, preferred_element_type=jnp.float32)  20.2 us
    all_gather x1, blocking collectives, local(): lax.all_gather(prompt_value, 'seq', axis=0, tiled=True)  15.4 us
    dot_general x4, matrix products, one_block(): jnp.einsum('hbl,ld->bhd', prob.astype(jnp.bfloat16), value_one, preferred...  13.8 us
  transfers between devices with their start and end apart: 10, of which 6 were waited for; matrix products, arithmetic and copies ran while one was open for 23% of the time, Pallas kernels for 0%

commit v1 on v0

v1 whole, which is shorter than its diff:
```python
import functools
import math

import jax
import jax.numpy as jnp
import numpy as np
from jax import lax
from jax.experimental import pallas as pl
from jax.experimental.pallas import tpu as pltpu
from jax.sharding import PartitionSpec as P

HD = 128
MESH = pl.DeviceIdType.MESH
N_Y = 4
N_SEQ = 4
N_SMP = 8
WINDOW = 4
LAG = 4
I1, J1, I2, J2, YA, YB, YC = 0, 1, 2, 3, 4, 6, 8


def dot_t(a, b):
    return lax.dot_general(a, b, (((1,), (1,)), ((), ())), preferred_element_type=jnp.float32)


def kernel(
    px_ref, sx_ref, wq_ref, wk_ref, wv_ref, qg_ref, kg_ref, freq_ref,
    out_ref, dec_ref,
    xb, w, proj, tabs, kvx, vaug, kvd, qbuf, acc, obuf, dsend, drecv,
    load_sem, send_sem, recv_sem, kv_send, kv_recv, o_sem, d_send, d_recv,
):
    rows = px_ref.shape[0]
    drows = sx_ref.shape[0]
    depth = wq_ref.shape[0]
    heads = wq_ref.shape[1] // HD
    slots = heads + 2
    count = rows + drows
    half = depth // 2
    quarter = depth // 4
    grp = lax.axis_index("grp")
    seq = lax.axis_index("seq")
    smp = lax.axis_index("smp")
    lo = grp // N_Y
    y = lax.rem(grp, N_Y)
    par = lax.rem(y, 2)
    up = lax.rem(seq + 1, N_SEQ)
    down = lax.rem(seq + N_SEQ - 1, N_SEQ)
    far = lax.rem(seq + 2, N_SEQ)
    near = lax.rem(seq + 2 * lo + N_SEQ - 1, N_SEQ)
    other = lax.rem(seq + N_SEQ + 1 - 2 * lo, N_SEQ)
    lo_grp = (1 - lo) * N_Y + y
    inter = (lo_grp, near, smp)
    intra = (lo_grp, seq, smp)
    y_up = lax.rem(y + 1, N_Y)
    y_down = lax.rem(y + N_Y - 1, N_Y)
    y_dev = ((lo * N_Y + y_up, seq, smp), (lo * N_Y + y_down, seq, smp))
    y_mine = (lo * N_Y + lax.rem(y + 1 + 2 * lo, N_Y), seq, smp)
    y_rest = (lo * N_Y + lax.rem(y + 3 - 2 * lo, N_Y), seq, smp)
    seq_dev = ((grp, up, smp), (grp, down, smp))

    loads = []
    loads.append(pltpu.make_async_copy(wk_ref, w.at[0, pl.ds(seq * depth, depth)], load_sem.at[0]))
    loads.append(pltpu.make_async_copy(wv_ref, w.at[1, pl.ds(seq * depth, depth)], load_sem.at[1]))
    for h in range(heads):
        loads.append(
            pltpu.make_async_copy(
                wq_ref.at[:, pl.ds(h * HD, HD)], w.at[2 + h, pl.ds(seq * depth, depth)], load_sem.at[2 + h]
            )
        )
    loads.append(pltpu.make_async_copy(px_ref, xb.at[pl.ds(0, rows)], load_sem.at[slots]))
    loads.append(pltpu.make_async_copy(sx_ref, xb.at[pl.ds(rows, drows)], load_sem.at[slots + 1]))
    for load in loads:
        load.start()

    barrier = pltpu.get_barrier_semaphore()
    for dev in (inter, intra) + y_dev + seq_dev:
        pl.semaphore_signal(barrier, inc=1, device_id=dev, device_id_type=MESH)
    for d in range(1, N_SMP):
        pl.semaphore_signal(
            barrier, inc=1, device_id=(grp, seq, lax.rem(smp + d, N_SMP)), device_id_type=MESH
        )
    pl.semaphore_wait(barrier, 6 + N_SMP - 1)

    def piece(slot, block, start, size):
        return w.at[slot, pl.ds(pl.multiple_of(block * depth + start, 16), size)]

    def message(slot, kind, block, start, size, dev):
        ref = piece(slot, block, start, size)
        return pltpu.make_async_remote_copy(
            src_ref=ref, dst_ref=ref, send_sem=send_sem.at[slot, kind], recv_sem=recv_sem.at[slot, kind],
            device_id=dev, device_id_type=MESH,
        )

    mine = par * half
    theirs = (1 - par) * half

    def send_i1(slot):
        message(slot, I1, seq, mine, half, inter).start()

    def send_y(slot, kind, block):
        for q in range(2):
            message(slot, kind + q, block, mine + q * quarter, quarter, y_dev[q]).start()

    def arrived(slot, kind, block, start, size):
        message(slot, kind, block, start, size, inter).wait_recv()

    for slot in range(WINDOW):
        loads[slot].wait()
        send_i1(slot)
    for slot in range(WINDOW, slots):
        loads[slot].wait()

    row = lax.broadcasted_iota(jnp.int32, (count, HD), 0)
    lane = lax.broadcasted_iota(jnp.int32, (count, HD), 1)
    position = jnp.where(row < rows, seq * rows + row, N_SEQ * rows + lax.rem(row - rows, 4))
    angle = position.astype(jnp.float32) * freq_ref[...]
    cosine = jnp.cos(angle)
    sine = jnp.sin(angle)
    sine = jnp.where(lane < HD // 2, -sine, sine)
    fold = HD ** (-0.5) * math.log2(math.e)
    for n, (gain_ref, factor) in enumerate(((kg_ref, 1.0), (qg_ref, fold))):
        gain = gain_ref[...] * factor
        tabs[n, 0] = cosine * gain
        tabs[n, 1] = sine * pltpu.roll(gain, HD // 2, 1)
    vaug[:, :, HD:] = jnp.ones((N_SEQ, rows, HD), jnp.bfloat16)
    kvd[1, :, HD:] = jnp.ones((drows, HD), jnp.bfloat16)
    loads[slots].wait()
    loads[slots + 1].wait()

    def rotated(n):
        u = proj[...]
        r = lax.rsqrt(jnp.mean(u * u, -1, keepdims=True) + 1e-6)
        return (r * (u * tabs[n, 0] + pltpu.roll(u, HD // 2, 1) * tabs[n, 1])).astype(jnp.bfloat16)

    def kv_message(n, src, dev):
        return pltpu.make_async_remote_copy(
            src_ref=src, dst_ref=src, send_sem=kv_send.at[n], recv_sem=kv_recv.at[n], device_id=dev, device_id_type=MESH
        )

    def kv_up():
        return kv_message(0, kvx.at[seq], seq_dev[0])

    def kv_down():
        return kv_message(1, kvx.at[seq], seq_dev[1])

    def kv_far_up():
        return kv_message(2, kvx.at[down, 0], seq_dev[0])

    def kv_far_down():
        return kv_message(3, kvx.at[up, 1], seq_dev[1])

    def out_copy(h):
        return pltpu.make_async_copy(
            obuf.at[h], out_ref.at[:, pl.ds(pl.multiple_of(h * HD, HD), HD)], o_sem.at[h]
        )

    def attend(h):
        q = qbuf[h, pl.ds(0, rows)]
        scores = dot_t(q, kvx[seq, 0])
        allowed = lax.broadcasted_iota(jnp.int32, (rows, rows), 1) <= lax.broadcasted_iota(jnp.int32, (rows, rows), 0)
        e = jnp.where(allowed, jnp.exp2(scores), 0.0).astype(jnp.bfloat16)
        acc[...] = jnp.dot(e, vaug[seq], preferred_element_type=jnp.float32)

        def block(j, _):
            p = jnp.exp2(dot_t(q, kvx[j, 0])).astype(jnp.bfloat16)
            acc[...] += jnp.dot(p, vaug[j], preferred_element_type=jnp.float32)
            return 0

        lax.fori_loop(0, seq, block, 0)
        obuf[h] = (acc[:, :HD] / acc[:, HD:]).astype(jnp.bfloat16)
        out_copy(h).start()

        qd = qbuf[h, pl.ds(rows, drows)]
        a = lax.broadcasted_iota(jnp.int32, (drows, drows), 0)
        b = lax.broadcasted_iota(jnp.int32, (drows, drows), 1)
        own = jnp.where((b <= a) & (a // 4 == b // 4), jnp.exp2(dot_t(qd, kvd[0, :, :HD])), 0.0)
        total = jnp.dot(own.astype(jnp.bfloat16), kvd[1], preferred_element_type=jnp.float32)
        for j in range(N_SEQ):
            p = jnp.exp2(dot_t(qd, kvx[j, 0])).astype(jnp.bfloat16)
            total += jnp.dot(p, vaug[j], preferred_element_type=jnp.float32)
        res = total[:, :HD] / total[:, HD:]
        dsend[:, :, pl.ds(pl.multiple_of(h * HD, HD), HD)] = res.reshape(N_SMP, drows // N_SMP, HD)

    first_att = LAG + 4

    def done_by(i):
        return jnp.clip(jnp.where(i > first_att, i - LAG - 1, jnp.where(i == first_att, 2, 0)), 0, heads)

    def step(i, _):
        @pl.when(i < slots)
        def _():
            arrived(i, I1, near, mine, half)
            message(i, J1, near, mine, half, intra).start()
            send_y(i, YA, near)

        @pl.when(i + WINDOW < slots)
        def _():
            send_i1(i + WINDOW)

        @pl.when((i >= 1) & (i - 1 < slots))
        def _():
            t = i - 1
            arrived(t, J1, other, mine, half)
            message(t, I2, other, mine + (1 - lo) * quarter, quarter, inter).start()
            send_y(t, YB, other)

        @pl.when((i >= 2) & (i - 2 < slots))
        def _():
            t = i - 2
            arrived(t, I2, far, mine + lo * quarter, quarter)
            message(t, J2, far, mine + lo * quarter, quarter, intra).start()
            message(t, YC + lo, far, mine + lo * quarter, quarter, y_mine).start()

        @pl.when((i >= 3) & (i - 3 < slots))
        def _():
            t = i - 3
            arrived(t, J2, far, mine + (1 - lo) * quarter, quarter)
            message(t, YC + 1 - lo, far, mine + (1 - lo) * quarter, quarter, y_rest).start()

        @pl.when(i == LAG + 2)
        def _():
            kv_up().wait_recv()
            kv_far_up().start()
            kv_down().wait_recv()
            kv_far_down().start()

        @pl.when(i >= LAG)
        def _():
            t = i - LAG
            for q in range(2):
                arrived(t, YA + q, near, theirs + q * quarter, quarter)
                arrived(t, YB + q, other, theirs + q * quarter, quarter)
                arrived(t, YC + q, far, theirs + q * quarter, quarter)
            proj[...] = jnp.dot(xb[...], w[t], preferred_element_type=jnp.float32)

            @pl.when(t == 0)
            def _():
                k = rotated(0)
                kvx[seq, 0] = k[:rows]
                kvd[0, :, :HD] = k[rows:]

            @pl.when(t == 1)
            def _():
                v = proj[...].astype(jnp.bfloat16)
                kvx[seq, 1] = v[:rows]
                kvd[1, :, :HD] = v[rows:]
                kv_up().start()
                kv_down().start()

            @pl.when(t >= 2)
            def _():
                qbuf[t - 2] = rotated(1)

        @pl.when(i == first_att)
        def _():
            kv_message(2, kvx.at[far, 0], seq_dev[0]).wait_recv()
            kv_message(3, kvx.at[far, 1], seq_dev[1]).wait_recv()
            vaug[:, :, :HD] = kvx[:, 1]

        def one(h, _):
            attend(h)
            return 0

        lax.fori_loop(done_by(i - 1), done_by(i), one, 0)
        return 0

    lax.fori_loop(0, slots + LAG, step, 0)

    def d_message(d, target):
        return pltpu.make_async_remote_copy(
            src_ref=dsend.at[target], dst_ref=drecv.at[smp], send_sem=d_send.at[d], recv_sem=d_recv.at[d],
            device_id=(grp, seq, target), device_id_type=MESH,
        )

    for d in range(1, N_SMP):
        d_message(d, lax.rem(smp + d, N_SMP)).start()
    drecv[smp] = dsend[smp]

    def sent(slot, _):
        for kind, size in ((I1, half), (J1, half), (I2, quarter), (J2, quarter)):
            message(slot, kind, seq, 0, size, inter).wait_send()
        for kind in range(YA, YC + 2):
            message(slot, kind, seq, 0, quarter, inter).wait_send()
        return 0

    lax.fori_loop(0, slots, sent, 0)
    kv_up().wait_send()
    kv_down().wait_send()
    kv_far_up().wait_send()
    kv_far_down().wait_send()
    for h in range(heads):
        out_copy(h).wait()
    for d in range(1, N_SMP):
        d_message(d, lax.rem(smp + d, N_SMP)).wait_send()
    for d in range(1, N_SMP):
        d_message(d, lax.rem(smp + N_SMP - d, N_SMP)).wait_recv()
    cols = heads * HD
    for j in range(N_SMP):
        dec_ref[:, j * cols : (j + 1) * cols] = drecv[j]


def local(prompt_x, sampled_x, w_query, w_key, w_value, q_gain, k_gain):
    rows, width = prompt_x.shape
    samples, steps, _ = sampled_x.shape
    drows = samples * steps
    depth, q_cols = w_query.shape
    heads = q_cols // HD
    slots = heads + 2
    count = rows + drows
    mine = drows // N_SMP
    half = np.arange(HD // 2, dtype=np.float64)
    freq = 1e6 ** (-2.0 * half / HD)
    freq = jnp.asarray(np.concatenate([freq, freq]).reshape(1, HD).astype(np.float32))
    any_spec = pl.BlockSpec(memory_space=pl.ANY)
    vmem = pl.BlockSpec(memory_space=pltpu.VMEM)
    prefill, dec = pl.pallas_call(
        kernel,
        out_shape=(
            jax.ShapeDtypeStruct((rows, q_cols), jnp.bfloat16),
            jax.ShapeDtypeStruct((mine, N_SMP * q_cols), jnp.float32),
        ),
        in_specs=[any_spec] * 5 + [vmem] * 3,
        out_specs=(any_spec, vmem),
        scratch_shapes=[
            pltpu.VMEM((count, width), jnp.bfloat16),
            pltpu.VMEM((slots, width, HD), jnp.bfloat16),
            pltpu.VMEM((count, HD), jnp.float32),
            pltpu.VMEM((2, 2, count, HD), jnp.float32),
            pltpu.VMEM((N_SEQ, 2, rows, HD), jnp.bfloat16),
            pltpu.VMEM((N_SEQ, rows, 2 * HD), jnp.bfloat16),
            pltpu.VMEM((2, drows, 2 * HD), jnp.bfloat16),
            pltpu.VMEM((heads, count, HD), jnp.bfloat16),
            pltpu.VMEM((rows, 2 * HD), jnp.float32),
            pltpu.VMEM((heads, rows, HD), jnp.bfloat16),
            pltpu.VMEM((N_SMP, mine, q_cols), jnp.float32),
            pltpu.VMEM((N_SMP, mine, q_cols), jnp.float32),
            pltpu.SemaphoreType.DMA((slots + 2,)),
            pltpu.SemaphoreType.DMA((slots, 10)),
            pltpu.SemaphoreType.DMA((slots, 10)),
            pltpu.SemaphoreType.DMA((4,)),
            pltpu.SemaphoreType.DMA((4,)),
            pltpu.SemaphoreType.DMA((heads,)),
            pltpu.SemaphoreType.DMA((N_SMP,)),
            pltpu.SemaphoreType.DMA((N_SMP,)),
        ],
        compiler_params=pltpu.CompilerParams(
            collective_id=0, has_side_effects=True, vmem_limit_bytes=48 * 2**20
        ),
    )(
        prompt_x, sampled_x.reshape(drows, width), w_query, w_key, w_value,
        q_gain.reshape(1, HD), k_gain.reshape(1, HD), freq,
    )
    return prefill, dec.astype(jnp.bfloat16).reshape(samples // N_SMP, steps, N_SMP * q_cols)


def solution(mesh):
    in_specs = (
        P(("grp", "seq"), None),
        P("grp", None, None),
        P("seq", "smp"),
        P("seq", "smp"),
        P("seq", "smp"),
        P(),
        P(),
    )
    out_specs = (P(("grp", "seq"), "smp"), P(("grp", "smp"), None, None))
    return jax.shard_map(local, mesh=mesh, in_specs=in_specs, out_specs=out_specs, check_vma=False)
```

time: 492 us -> 130 us (0.26)
  waiting for transfers between devices: 266 us -> 0 us
  Pallas kernels: 0 us -> 120 us
  matrix products: 69.7 us -> 0 us
  blocking collectives: 66.5 us -> 0 us
  starting transfers between devices: 25 us -> 0 us
  local copies, waits for them, and re-layouts: 30.1 us -> 8.84 us
  between operations: 14.1 us -> 0.67 us
  other arithmetic: 13.3 us -> 0.02 us
    all_gather x5 -> x0, waiting for transfers between devices: 244 us -> none  [the longest x1 183 us: local(): lax.all_gather(w_query, 'seq', axis=0, tiled=True)]
    pallas_call x0 -> x1, Pallas kernels: none -> 120 us  [local(): pl.pallas_call(kernel, out_shape=(jax.ShapeDtypeStruct((rows, q_cols), jn...]
    all_gather x2 -> x0, blocking collectives: 66.5 us -> none  [the longest x1 51.1 us: local(): lax.all_gather(prompt_key, 'seq', axis=0, tiled=True)]
    dot_general x11 -> x0, matrix products: 45.8 us -> none  [the longest x3 20.2 us: local(): jnp.dot(inputs, piece, preferred_element_type=jnp.float32)]
    all_to_all x5 -> x0, starting transfers between devices: 24.9 us -> none  [the longest x1 5.72 us: local(): lax.all_to_all(dec_value, 'smp', split_axis=0, concat_axis=1, tiled=True)]
    sub x4 -> x0, matrix products: 23.8 us -> none  [one_block(): prob = jnp.where(allowed, jnp.exp(scores - top), 0.0)]
    all_to_all x5 -> x0, waiting for transfers between devices: 19.6 us -> none  [the longest x1 11.7 us: local(): lax.all_to_all(attended, 'seq', split_axis=0, concat_axis=1, tiled=True)]
    dynamic_slice x8 -> x0, local copies, waits for them, and re-layouts: 5.47 us -> none  [the longest x4 4.72 us: local(): lax.map(one_block, jnp.arange(length // block, dtype=jnp.int32))]
  transfers between devices with their start and end apart: 10 -> 0, of which waited for: 6 -> 0; matrix products, arithmetic and copies ran while one was open for 23% -> 0% of each run, Pallas kernels for 0% -> 0%
where the time goes in v1:
time: 130 us; the launch traced here: 129 us
  Pallas kernels  120 us (92%)
  local copies, waits for them, and re-layouts  8.84 us (7%)
    pallas_call x1, Pallas kernels, local(): pl.pallas_call(kernel, out_shape=(jax.ShapeDtypeStruct((rows, q_cols), jn...  120 us
    unnamed x13, local copies, waits for them, and re-layouts  6.61 us

profile of v1, /device:TPU:1, one launch (start us, length us, event | category | flops | bytes accessed | tf_op | source)
XLA Modules:
  0.0 129.1 jit_solution(13746849691077467475)
XLA Ops:
  0.6 1.5 %reshape.16.sx_ref = bf16[64,5120]{1,0:T(8,128)(2,1)S(1)} reshape(bf16[16,4,5120]{2,1,0:T(4,128)(2,1)} %param.9) | data formatting | bytes 1310720 | tf_op jit(solution)/shard_map/reshape | solution.py:350
  2.1 0.0 copy-start
  2.2 1.7 %copy-done = bf16[1280,1024]{1,0:T(8,128)(2,1)S(1)} copy-done((bf16[1280,1024]{1,0:T(8,128)(2,1)S(1)}, bf16[1280,1024]{1,0:T(8,128)(2,1)}, u32[]{:S(2)}) %copy-start) | copy-done | bytes 2621464
  3.9 0.0 copy-start.1
  3.9 1.0 copy-done.1
  4.9 0.0 copy-start.2
  4.9 1.0 copy-done.2
  5.8 0.0 copy-start.3
  5.8 0.7 copy-done.3
  6.5 0.0 copy-start.4
  6.5 0.7 copy-done.4
  7.2 0.0 copy-start.5
  7.2 0.7 copy-done.5
  7.8 119.6 %shard_map.95 = (bf16[512,1024]{1,0:T(8,128)(2,1)S(1)}, f32[8,8192]{1,0:T(8,128)S(1)}) custom-call(bf16[512,5120]{1,0:T(8,128)(2,1)} %px_ref.1, bf16[64,5120]{1,0:T(8,128)(2,1)S(1)} %reshape.16.sx_ref, bf16[1280,1024]{1,0:T(8,128)(2,1)S(1)} %copy-done, bf16[1280,128]{1,0:T(8,128)(2,1)S(1)} %copy-done.1, bf16[1280,128]{1,0:T(8,128)(2,1)S(1)} %copy-done.2, ...), custom_call_target="tpu_custom_call" | custom-call | tf_op jit(solution)/shard_map/pallas_call | solution.py:316
  127.4 0.7 reshape.19
  128.1 1.0 copy.11
  (1 shorter events, 0.0 us)
Async XLA Ops:
  2.1 1.7 %copy-start = (bf16[1280,1024]{1,0:T(8,128)(2,1)S(1)}, bf16[1280,1024]{1,0:T(8,128)(2,1)}, u32[]{:S(2)}) copy-start(bf16[1280,1024]{1,0:T(8,128)(2,1)} %wq_ref.1) | copy-start | bytes 7864324
  3.9 1.0 copy-start.1
  4.9 1.0 copy-start.2
  5.8 0.7 copy-start.3
  6.5 0.7 copy-start.4
  7.2 0.7 copy-start.5

commit v2 on v1

v2 whole, which is shorter than its diff:
```python
import math

import jax
import jax.numpy as jnp
from jax import lax
from jax.experimental import pallas as pl
from jax.experimental.pallas import tpu as pltpu
from jax.sharding import PartitionSpec as P

HD = 128
PAIR = 2 * HD
MESH = pl.DeviceIdType.MESH
N_Y = 4
N_SEQ = 4
N_SMP = 8
N_X = N_SMP // 2
SUBS = 5
X_CUTS = 4
WINDOW = 2
AT_J1 = 1
AT_I2 = 2
AT_J2 = 3
LAG = 5
KV_ON = 13
KV_END = 15
X_START = (3, 5, 7, 9)
X_STEPS = (11, 15, 19, 23, 16, 20, 24, 27, 28, 30)
PARTNER_AT = (15, 15, 16, 16, 16, 17, 17, 18, 18, 19)
ATTEND_AT = (15, 16, 19, 19, 19, 19, 19, 19)
I1, J1, I2, J2, Y = 0, 1, 2, 3, 4


def reached(i, steps):
    return sum((i >= step).astype(jnp.int32) for step in steps)


def chunk_at(i):
    third, rest = i // 3, lax.rem(i, 3)
    return jnp.where(i < SUBS + SUBS // 2, jnp.where(rest == 2, SUBS + third, 2 * third + rest), i)


def dot(a, b):
    return jnp.dot(a, b, preferred_element_type=jnp.float32)


def dot_t(a, b):
    return lax.dot_general(a, b, (((1,), (1,)), ((), ())), preferred_element_type=jnp.float32)


def kernel(
    px_ref, sx_ref, wq_ref, wk_ref, wv_ref, qg_ref, kg_ref,
    out_ref, dout_ref,
    xb, xp, sxb, w, proj, projp, qsend, tabs, gains, kvx, vaug, kvd, qbuf, obuf, dsend, dec_ref,
    load_sem, x_sem, o_sem, send_sem, recv_sem, kv_send, kv_recv, d_send, d_recv, xs_send, xs_recv, q_send, q_recv,
):
    rows = px_ref.shape[0]
    drows = sx_ref.shape[0] * sx_ref.shape[1]
    heads = wq_ref.shape[1] // HD
    shared = heads // 2
    depth = wq_ref.shape[0] // SUBS
    width = N_SEQ * depth
    chunks = SUBS * (1 + shared // 2)
    count = rows + drows
    half = depth // 2
    quarter = depth // 4
    grp = lax.axis_index("grp")
    seq = lax.axis_index("seq")
    smp = lax.axis_index("smp")
    lo = grp // N_Y
    y = lax.rem(grp, N_Y)
    par = lax.rem(y, 2)
    up = lax.rem(seq + 1, N_SEQ)
    down = lax.rem(seq + N_SEQ - 1, N_SEQ)
    far = lax.rem(seq + 2, N_SEQ)
    mirror = N_SEQ - 1 - seq
    near = lax.rem(seq + 2 * lo + N_SEQ - 1, N_SEQ)
    other = lax.rem(seq + N_SEQ + 1 - 2 * lo, N_SEQ)
    lo_grp = (1 - lo) * N_Y + y
    inter = (lo_grp, near, smp)
    intra = (lo_grp, seq, smp)
    y_up = lax.rem(y + 1, N_Y)
    y_down = lax.rem(y + N_Y - 1, N_Y)
    y_dev = ((lo * N_Y + y_up, seq, smp), (lo * N_Y + y_down, seq, smp))
    side = lax.rem((y + 1) // 2, 2)
    pair = (lo * N_Y + y + 1 - 2 * par, seq, smp)
    ext = (lo * N_Y + lax.rem(y + 2 * par + N_Y - 1, N_Y), seq, smp)
    core = lax.rem(smp, 2)
    x_up = lax.rem(smp // 2 + 1, N_X) * 2 + core
    x_down = lax.rem(smp // 2 + N_X - 1, N_X) * 2 + core
    x_far = lax.rem(smp // 2 + 2, N_X) * 2 + core
    x_dev = ((grp, seq, x_up), (grp, seq, x_down))
    core_dev = (grp, seq, smp + 1 - 2 * core)
    seq_dev = ((grp, up, smp), (grp, down, smp))

    native = pl.ds(pl.multiple_of(seq * depth, 16), depth)
    for c in range(chunks):
        p, part = c // SUBS, pl.ds(c % SUBS * depth, depth)
        if p == 0:
            for n, ref in enumerate((wk_ref, wv_ref)):
                pltpu.make_async_copy(
                    ref.at[part], w.at[c, native, pl.ds(n * HD, HD)], load_sem.at[0]
                ).start()
        else:
            col = pl.multiple_of((side * shared + 2 * p - 2) * HD, HD)
            pltpu.make_async_copy(
                wq_ref.at[part, pl.ds(col, PAIR)], w.at[c, native], load_sem.at[1]
            ).start()
    x_loads = [
        pltpu.make_async_copy(sx_ref, sxb, x_sem.at[0]),
        pltpu.make_async_copy(qg_ref, gains.at[1], x_sem.at[1]),
        pltpu.make_async_copy(kg_ref, gains.at[0], x_sem.at[1]),
    ]
    for sub in range(SUBS):
        for j in range(N_SEQ):
            x_loads.append(
                pltpu.make_async_copy(
                    px_ref.at[:, pl.ds((j * SUBS + sub) * depth, depth)],
                    xb.at[pl.ds(0, rows), pl.ds(sub * width + j * depth, depth)],
                    x_sem.at[2],
                )
            )
    for load in x_loads:
        load.start()

    barrier = pltpu.get_barrier_semaphore()
    for dev in (inter, intra) + y_dev + seq_dev:
        pl.semaphore_signal(barrier, inc=1, device_id=dev, device_id_type=MESH)
    for d in range(1, N_SMP):
        for s in (seq, mirror):
            pl.semaphore_signal(
                barrier, inc=1, device_id=(grp, s, lax.rem(smp + d, N_SMP)), device_id_type=MESH
            )
    pl.semaphore_wait(barrier, 6 + 2 * (N_SMP - 1))

    def message(c, kind, block, start, size, dev):
        ref = w.at[c, pl.ds(pl.multiple_of(block * depth + start, 16), size)]
        return pltpu.make_async_remote_copy(
            src_ref=ref, dst_ref=ref, send_sem=send_sem.at[kind], recv_sem=recv_sem.at[c, kind],
            device_id=dev, device_id_type=MESH,
        )

    mine = par * half
    theirs = (1 - par) * half

    def send_i1(c):
        for n, (first, last) in enumerate(((0, SUBS), (SUBS, chunks))):
            @pl.when(c == first)
            def _(n=n, first=first, last=last):
                ref = w.at[pl.ds(first, last - first), native]
                pltpu.make_async_copy(ref, ref, load_sem.at[n]).wait()

        message(c, I1, seq, mine, half, inter).start()

    def send_y(c, block, q):
        start = mine + q * quarter

        @pl.when(c < SUBS)
        def _():
            for n in range(2):
                @pl.when(q == n)
                def _():
                    message(c, Y, block, start, quarter, y_dev[n]).start()

        @pl.when(c >= SUBS)
        def _():
            message(c, Y, block, start, quarter, ext).start()

    def arrived(c, kind, block, start, size):
        message(c, kind, block, start, size, inter).wait_recv()

    for c in range(WINDOW):
        send_i1(chunk_at(jnp.int32(c)))

    rblock = count // X_CUTS
    share = SUBS * width // N_SMP

    core_sem = 4 * X_CUTS

    def x_message(n, buf, m, r, dev):
        at = (pl.ds(r * rblock, rblock), pl.ds(pl.multiple_of(m * share, HD), share))
        return pltpu.make_async_remote_copy(
            src_ref=buf.at[at], dst_ref=xp.at[at], send_sem=xs_send, recv_sem=xs_recv.at[n],
            device_id=dev, device_id_type=MESH,
        )

    def x_pair(r):
        return x_message(r, xb, smp, r, pair)

    def x_ring(way, r):
        return x_message((1 + way) * X_CUTS + r, xp, smp, r, x_dev[way])

    def x_fwd(way, r):
        return x_message(3 * X_CUTS + r, xp, (x_down, x_up)[way], r, x_dev[way])

    def x_core(k, r):
        return x_message(core_sem, xp, (smp, x_down, x_up, x_far)[k], r, core_dev)

    def x_step(n):
        stage, r = n // X_CUTS, n % X_CUTS
        if stage == 0:
            x_pair(r).wait_recv()
            x_ring(0, r).start()
            x_ring(1, r).start()
            x_core(0, r).start()
        elif stage == 1:
            for way in range(2):
                x_ring(way, r).wait_recv()
                if r // 2 == way:
                    x_fwd(way, r).start()
                x_core(1 + way, r).start()
        else:
            for way in range(2):
                x_fwd(way, 2 * way + r).wait_recv()
                x_core(3, 2 * way + r).start()

    def x_finish():
        ref = xp.at[:, pl.ds(0, N_X * share)]
        pltpu.make_async_copy(ref, ref, xs_recv.at[core_sem]).wait()

    def x_sent():
        pltpu.make_async_copy(xp, xp, xs_send).wait()

    def start_x():
        for n, ref in enumerate((sxb, gains, xb.at[pl.ds(0, rows)])):
            pltpu.make_async_copy(ref, ref, x_sem.at[n]).wait()
        for sub in range(SUBS):
            for j in range(N_SEQ):
                cols = (j * SUBS + sub) * depth
                at = sub * width + j * depth
                xb[rows:, at : at + depth] = sxb[:, :, cols : cols + depth].reshape(drows, depth)

    def prepare():
        row = lax.broadcasted_iota(jnp.int32, (count, HD), 0)
        lane = lax.broadcasted_iota(jnp.int32, (count, HD), 1)
        index = lax.rem(lane, HD // 2).astype(jnp.float32)
        freq = jnp.exp(index * (-2.0 * math.log(1e6) / HD))
        position = jnp.where(row < rows, seq * rows + row, N_SEQ * rows + lax.rem(row - rows, 4))
        angle = position.astype(jnp.float32) * freq
        cosine = jnp.cos(angle)
        sine = jnp.sin(angle)
        sine = jnp.where(lane < HD // 2, -sine, sine)
        fold = HD ** (-0.5) * math.log2(math.e)
        for n, factor in enumerate((1.0, fold)):
            gain = gains[n] * factor
            tabs[n, 0] = cosine * gain
            tabs[n, 1] = sine * pltpu.roll(gain, HD // 2, 1)
        vaug[:, :, HD:] = jnp.ones((N_SEQ, rows, HD), jnp.bfloat16)
        kvd[1, :, HD:] = jnp.ones((drows, HD), jnp.bfloat16)

    def rotated(n, u):
        r = lax.rsqrt(jnp.mean(u * u, -1, keepdims=True) + 1e-6)
        return (r * (u * tabs[n, 0] + pltpu.roll(u, HD // 2, 1) * tabs[n, 1])).astype(jnp.bfloat16)

    def kv_message(n, src, dev):
        return pltpu.make_async_remote_copy(
            src_ref=src, dst_ref=src, send_sem=kv_send, recv_sem=kv_recv.at[n], device_id=dev, device_id_type=MESH
        )

    def kv_own(part, way):
        return kv_message(0, kvx.at[seq, part], seq_dev[way])

    def kv_far(part):
        return kv_message(1, kvx.at[(down, up)[part], part], seq_dev[part])

    def kv_wait(n, blocks):
        ref = kvx.at[pl.ds(0, blocks)]
        pltpu.make_async_copy(ref, ref, (kv_recv.at[0], kv_recv.at[1], kv_send)[n]).wait()

    def out_copy(h):
        return pltpu.make_async_copy(
            obuf.at[h], out_ref.at[:, pl.ds(pl.multiple_of(h * HD, HD), HD)], o_sem
        )

    tile = rows // 2

    def attend_blocks(h, full):
        for r in range(2):
            q = qbuf[h, pl.ds(r * tile, tile)]
            e = jnp.exp2(dot_t(q, kvx[full, 0, pl.ds(r * tile, tile)]))
            allowed = lax.broadcasted_iota(jnp.int32, (tile, tile), 1) <= lax.broadcasted_iota(
                jnp.int32, (tile, tile), 0
            )
            e = jnp.where(allowed, e, 0.0).astype(jnp.bfloat16)
            total = dot(e, vaug[full, pl.ds(r * tile, tile)])
            if r > 0:
                e = jnp.exp2(dot_t(q, kvx[full, 0, pl.ds(0, tile)])).astype(jnp.bfloat16)
                total += dot(e, vaug[full, pl.ds(0, tile)])
            for j in range(full):
                e = jnp.exp2(dot_t(q, kvx[j, 0])).astype(jnp.bfloat16)
                total += dot(e, vaug[j])
            obuf[h, pl.ds(r * tile, tile)] = (total[:, :HD] / total[:, HD:]).astype(jnp.bfloat16)

    def attend_samples(h):
        q = qbuf[h, pl.ds(rows, drows)]
        a = lax.broadcasted_iota(jnp.int32, (drows, drows), 0)
        b = lax.broadcasted_iota(jnp.int32, (drows, drows), 1)
        own = jnp.where((b <= a) & (a // 4 == b // 4), jnp.exp2(dot_t(q, kvd[0, :, :HD])), 0.0)
        total = dot(own.astype(jnp.bfloat16), kvd[1])
        for j in range(N_SEQ):
            total += dot(jnp.exp2(dot_t(q, kvx[j, 0])).astype(jnp.bfloat16), vaug[j])
        res = total[:, :HD] / total[:, HD:]
        dsend[:, :, pl.ds(pl.multiple_of(h * HD, HD), HD)] = res.reshape(N_SMP, drows // N_SMP, HD)

    def attend(h):
        for full in range(N_SEQ):
            @pl.when(seq == full)
            def _(full=full):
                attend_blocks(h, full)

        out_copy(h).start()

    cols = heads * HD

    def d_message(g, n, to_seq, target):
        first = jnp.where(g < shared // 2, side, 1 - side) * shared + lax.rem(g, shared // 2) * 2
        col = pl.multiple_of(first * HD, HD)
        return pltpu.make_async_remote_copy(
            src_ref=dsend.at[target, :, pl.ds(col, PAIR)],
            dst_ref=dec_ref.at[:, pl.ds(pl.multiple_of(smp * cols + col, HD), PAIR)],
            send_sem=d_send.at[n], recv_sem=d_recv.at[n],
            device_id=(grp, to_seq, target), device_id_type=MESH,
        )

    def q_message(j):
        return pltpu.make_async_remote_copy(
            src_ref=qsend.at[j], dst_ref=qbuf.at[side * shared + j], send_sem=q_send, recv_sem=q_recv.at[j],
            device_id=pair, device_id_type=MESH,
        )

    def x_cols(sub):
        return pl.ds(pl.multiple_of(sub * width, HD), width)

    def accumulate(ref, x_ref, c):
        sub = lax.rem(c, SUBS)
        part = dot(x_ref[:, x_cols(sub)], w[c])

        @pl.when(sub == 0)
        def _():
            ref[...] = part

        @pl.when(sub > 0)
        def _():
            ref[...] += part

    def partner(n, _):
        accumulate(projp, xp, SUBS + n)

        @pl.when(lax.rem(n, SUBS) == SUBS - 1)
        def _():
            for k in range(2):
                j = n // SUBS * 2 + k
                qsend[j] = rotated(1, projp[:, k * HD : (k + 1) * HD])
                q_message(j).start()

        return 0

    def one(n, _):
        g = n // 2
        received = g >= shared // 2
        j = lax.rem(g, shared // 2) * 2
        first = jnp.where(received, 1 - side, side) * shared + j
        opening = lax.rem(n, 2) == 0

        @pl.when(opening & received)
        def _():
            q_message(j).wait_recv()
            q_message(j + 1).wait_recv()

        @pl.when(opening & ((seq < N_SEQ // 2) | (g == shared - 1)))
        def _():
            attend_samples(first)
            attend_samples(first + 1)
            for d in range(1, N_SMP):
                d_message(g, 0, seq, lax.rem(smp + d, N_SMP)).start()

        @pl.when(opening & (seq < N_SEQ // 2) & (g < shared - 1))
        def _():
            for d in range(N_SMP):
                d_message(g, 1, mirror, lax.rem(smp + d, N_SMP)).start()

        attend(first + lax.rem(n, 2))
        return 0

    def x_place(place):
        @pl.when((place >= min(X_STEPS)) & (place <= max(X_STEPS)))
        def _():
            for n, at in enumerate(X_STEPS):
                @pl.when(place == at)
                def _(n=n):
                    x_step(n)

    def step(i, _):
        t = chunk_at(i - LAG)
        new = chunk_at(i)

        @pl.when(i < chunks)
        def _():
            arrived(new, I1, near, mine, half)
            message(new, J1, near, mine, half, intra).start()
            for q in range(2):
                send_y(new, near, q)

        @pl.when(i + WINDOW < chunks)
        def _():
            send_i1(chunk_at(i + WINDOW))

        @pl.when(i == 0)
        def _():
            start_x()

        for n, at in enumerate(X_START):
            @pl.when(i == at)
            def _(n=n):
                x_pair(n).start()

        @pl.when((i >= AT_J1) & (i - AT_J1 < chunks))
        def _():
            c = chunk_at(i - AT_J1)
            arrived(c, J1, other, mine, half)
            message(c, I2, other, mine + (1 - lo) * quarter, quarter, inter).start()
            for q in range(2):
                send_y(c, other, q)

        x_place(2 * i)

        @pl.when((i >= AT_I2) & (i - AT_I2 < chunks))
        def _():
            c = chunk_at(i - AT_I2)
            arrived(c, I2, far, mine + lo * quarter, quarter)
            message(c, J2, far, mine + lo * quarter, quarter, intra).start()
            send_y(c, far, lo)

        @pl.when((i >= AT_J2) & (i - AT_J2 < chunks))
        def _():
            c = chunk_at(i - AT_J2)
            arrived(c, J2, far, mine + (1 - lo) * quarter, quarter)
            send_y(c, far, 1 - lo)

        @pl.when(i == 1)
        def _():
            prepare()

        @pl.when(i == KV_ON)
        def _():
            kv_wait(0, 2)
            for part in range(2):
                kv_far(part).start()

        active = i >= LAG

        @pl.when(active)
        def _():
            message(t, Y, 0, 0, 3 * half, inter).wait_recv()

        x_place(2 * i + 1)

        @pl.when(i == PARTNER_AT[0])
        def _():
            x_finish()

        lax.fori_loop(reached(i - 1, PARTNER_AT), reached(i, PARTNER_AT), partner, 0)

        @pl.when(active)
        def _():
            accumulate(proj.at[jnp.minimum(t // SUBS, 1)], xb, t)

            @pl.when(t == SUBS - 1)
            def _():
                k = rotated(0, proj[0, :, :HD])
                v = proj[0, :, HD:].astype(jnp.bfloat16)
                kvx[seq, 0] = k[:rows]
                kvx[seq, 1] = v[:rows]
                kvd[0, :, :HD] = k[rows:]
                kvd[1, :, :HD] = v[rows:]
                for part in range(2):
                    for way in range(2):
                        kv_own(part, way).start()

            @pl.when((t >= SUBS) & (lax.rem(t, SUBS) == SUBS - 1))
            def _():
                for k in range(2):
                    qbuf[side * shared + (t // SUBS - 1) * 2 + k] = rotated(1, proj[1, :, k * HD : (k + 1) * HD])

        @pl.when(i == KV_END)
        def _():
            kv_wait(1, 1)
            vaug[:, :, :HD] = kvx[:, 1]

        lax.fori_loop(reached(i - 1, ATTEND_AT), reached(i, ATTEND_AT), one, 0)
        return 0

    lax.fori_loop(0, chunks + LAG, step, 0)

    @pl.when(seq < N_SEQ // 2)
    def _():
        dec_ref[:, pl.ds(pl.multiple_of(smp * cols, HD), cols)] = dsend[smp]

    @pl.when(seq >= N_SEQ // 2)
    def _():
        col = pl.multiple_of((1 - side) * shared * HD + (shared - 2) * HD, HD)
        dec_ref[:, pl.ds(pl.multiple_of(smp * cols + col, HD), PAIR)] = dsend[smp, :, pl.ds(col, PAIR)]

    for kind, size in ((I1, half), (J1, half), (I2, quarter), (J2, quarter), (Y, 3 * half)):
        ref = w.at[:, pl.ds(0, size)]
        pltpu.make_async_remote_copy(
            src_ref=ref, dst_ref=ref, send_sem=send_sem.at[kind], recv_sem=recv_sem.at[0, kind],
            device_id=inter, device_id_type=MESH,
        ).wait_send()
    x_sent()
    pltpu.make_async_copy(qsend, qsend, q_send).wait()
    kv_wait(2, 3)
    pltpu.make_async_copy(obuf, obuf, o_sem).wait()

    early = dsend.at[:, :, pl.ds(0, cols - PAIR)]

    @pl.when(seq < N_SEQ // 2)
    def _():
        part = dsend.at[pl.ds(0, N_SMP - 1)]
        pltpu.make_async_copy(early, early, d_send.at[1]).wait()
        pltpu.make_async_copy(part, part, d_send.at[0]).wait()
        pltpu.make_async_copy(part, part, d_recv.at[0]).wait()

    @pl.when(seq >= N_SEQ // 2)
    def _():
        part = dsend.at[pl.ds(0, N_SMP - 1), :, pl.ds(0, PAIR)]
        pltpu.make_async_copy(part, part, d_send.at[0]).wait()
        pltpu.make_async_copy(early, early, d_recv.at[1]).wait()
        pltpu.make_async_copy(part, part, d_recv.at[0]).wait()

    dout_ref[...] = dec_ref[...].astype(jnp.bfloat16)


def local(prompt_x, sampled_x, w_query, w_key, w_value, q_gain, k_gain):
    rows, width = prompt_x.shape
    samples, steps, _ = sampled_x.shape
    drows = samples * steps
    q_cols = w_query.shape[1]
    heads = q_cols // HD
    shared = heads // 2
    chunks = SUBS * (1 + shared // 2)
    count = rows + drows
    mine = drows // N_SMP
    hbm = pl.BlockSpec(memory_space=pltpu.HBM)
    vmem = pl.BlockSpec(memory_space=pltpu.VMEM)
    dma = pltpu.SemaphoreType.DMA
    prefill, dec = pl.pallas_call(
        kernel,
        out_shape=(
            jax.ShapeDtypeStruct((rows, q_cols), jnp.bfloat16),
            jax.ShapeDtypeStruct((mine, N_SMP * q_cols), jnp.bfloat16),
        ),
        in_specs=[hbm] * 7,
        out_specs=(pl.BlockSpec(memory_space=pl.ANY), vmem),
        scratch_shapes=[
            pltpu.VMEM((count, width), jnp.bfloat16),
            pltpu.VMEM((count, width), jnp.bfloat16),
            pltpu.VMEM((samples, steps, width), jnp.bfloat16),
            pltpu.VMEM((chunks, width // SUBS, PAIR), jnp.bfloat16),
            pltpu.VMEM((2, count, PAIR), jnp.float32),
            pltpu.VMEM((count, PAIR), jnp.float32),
            pltpu.VMEM((shared, count, HD), jnp.bfloat16),
            pltpu.VMEM((2, 2, count, HD), jnp.float32),
            pltpu.VMEM((2, 1, HD), jnp.float32),
            pltpu.VMEM((N_SEQ, 2, rows, HD), jnp.bfloat16),
            pltpu.VMEM((N_SEQ, rows, PAIR), jnp.bfloat16),
            pltpu.VMEM((2, drows, PAIR), jnp.bfloat16),
            pltpu.VMEM((heads, count, HD), jnp.bfloat16),
            pltpu.VMEM((heads, rows, HD), jnp.bfloat16),
            pltpu.VMEM((N_SMP, mine, q_cols), jnp.float32),
            pltpu.VMEM((mine, N_SMP * q_cols), jnp.float32),
            dma((2,)),
            dma((3,)),
            dma,
            dma((5,)),
            dma((chunks, 5)),
            dma,
            dma((2,)),
            dma((2,)),
            dma((2,)),
            dma,
            dma((4 * X_CUTS + 1,)),
            dma,
            dma((shared,)),
        ],
        compiler_params=pltpu.CompilerParams(
            collective_id=0, has_side_effects=True, vmem_limit_bytes=58 * 2**20
        ),
    )(prompt_x, sampled_x, w_query, w_key, w_value, q_gain.reshape(1, HD), k_gain.reshape(1, HD))
    return prefill, dec.reshape(samples // N_SMP, steps, N_SMP * q_cols)


def solution(mesh):
    in_specs = (
        P(("grp", "seq"), None),
        P("grp", None, None),
        P("seq", "smp"),
        P("seq", "smp"),
        P("seq", "smp"),
        P(),
        P(),
    )
    out_specs = (P(("grp", "seq"), "smp"), P(("grp", "smp"), None, None))
    return jax.shard_map(local, mesh=mesh, in_specs=in_specs, out_specs=out_specs, check_vma=False)
```

time: 130 us -> 103 us (0.79)
  Pallas kernels: 120 us -> 98.4 us
  local copies, waits for them, and re-layouts: 8.84 us -> 3.88 us
    pallas_call x1, Pallas kernels: 120 us -> 98.4 us  [local(): pl.pallas_call(kernel, out_shape=(jax.ShapeDtypeStruct((rows, q_cols), jn...]
    unnamed x13 -> x1, local copies, waits for them, and re-layouts: 6.61 us -> 2.26 us
where the time goes in v2:
time: 103 us
  Pallas kernels  98.4 us (96%)
  local copies, waits for them, and re-layouts  3.88 us (4%)
    pallas_call x1, Pallas kernels, local(): pl.pallas_call(kernel, out_shape=(jax.ShapeDtypeStruct((rows, q_cols), jn...  98.4 us
    unnamed x1, local copies, waits for them, and re-layouts  2.26 us

profile of v2, /device:TPU:1, one launch (start us, length us, event | category | flops | bytes accessed | tf_op | source)
XLA Modules:
  0.0 102.9 jit_solution(4857741770724101377)
XLA Ops:
  0.6 98.4 %shard_map.86 = (bf16[512,1024]{1,0:T(8,128)(2,1)}, bf16[8,8192]{1,0:T(8,128)(2,1)}) custom-call(bf16[512,5120]{1,0:T(8,128)(2,1)} %px_ref.1, bf16[16,4,5120]{2,1,0:T(4,128)(2,1)} %sx_ref.1, bf16[1280,1024]{1,0:T(8,128)(2,1)} %wq_ref.1, bf16[1280,128]{1,0:T(8,128)(2,1)} %wk_ref.1, bf16[1280,128]{1,0:T(8,128)(2,1)} %wv_ref.1, f32[1,128]{1,0:T(1,128)} %bitcast.2, ...), custom_call_target="tpu_custom_call" | custom-call | tf_op jit(solution)/shard_map/pallas_call | solution.py:546
  99.0 1.6 %reshape.15 = bf16[2,4,8192]{2,1,0:T(4,128)(2,1)} reshape(bf16[8,8192]{1,0:T(8,128)(2,1)} %get-tuple-element.5) | data formatting | bytes 262144 | tf_op jit(solution)/shard_map/reshape | solution.py:589
  100.7 2.3 %copy.10 = bf16[512,1024]{1,0:T(8,128)(2,1)} copy(bf16[512,1024]{1,0:T(8,128)(2,1)} %get-tuple-element.8) | data formatting | bytes 2097152

commit v3 on v2

--- a/solution.py
+++ b/solution.py
@@ -17,16 +17,17 @@
 SUBS = 5
 X_CUTS = 4
 WINDOW = 2
+OUT_CUTS = 4
 AT_J1 = 1
 AT_I2 = 2
 AT_J2 = 3
 LAG = 5
-KV_ON = 13
-KV_END = 15
+KV_ON = 12
+KV_END = 14
 X_START = (3, 5, 7, 9)
 X_STEPS = (11, 15, 19, 23, 16, 20, 24, 27, 28, 30)
 PARTNER_AT = (15, 15, 16, 16, 16, 17, 17, 18, 18, 19)
-ATTEND_AT = (15, 16, 19, 19, 19, 19, 19, 19)
+ATTEND_AT = (19, 19, 19, 19, 19, 19, 19, 19)
 I1, J1, I2, J2, Y = 0, 1, 2, 3, 4
 
 
@@ -35,8 +36,7 @@
 
 
 def chunk_at(i):
-    third, rest = i // 3, lax.rem(i, 3)
-    return jnp.where(i < SUBS + SUBS // 2, jnp.where(rest == 2, SUBS + third, 2 * third + rest), i)
+    return jnp.where((i < 3) | (i > 5), i, jnp.where(i == 3, SUBS, i - 1))
 
 
 def dot(a, b):
@@ -299,7 +299,7 @@
         for j in range(N_SEQ):
             total += dot(jnp.exp2(dot_t(q, kvx[j, 0])).astype(jnp.bfloat16), vaug[j])
         res = total[:, :HD] / total[:, HD:]
-        dsend[:, :, pl.ds(pl.multiple_of(h * HD, HD), HD)] = res.reshape(N_SMP, drows // N_SMP, HD)
+        dsend[:, :, :, pl.ds(pl.multiple_of(h * HD, HD), HD)] = res.reshape(dsend.shape[:3] + (HD,))
 
     def attend(h):
         for full in range(N_SEQ):
@@ -315,8 +315,8 @@
         first = jnp.where(g < shared // 2, side, 1 - side) * shared + lax.rem(g, shared // 2) * 2
         col = pl.multiple_of(first * HD, HD)
         return pltpu.make_async_remote_copy(
-            src_ref=dsend.at[target, :, pl.ds(col, PAIR)],
-            dst_ref=dec_ref.at[:, pl.ds(pl.multiple_of(smp * cols + col, HD), PAIR)],
+            src_ref=dsend.at[target, :, :, pl.ds(col, PAIR)],
+            dst_ref=dec_ref.at[:, :, pl.ds(pl.multiple_of(smp * cols + col, HD), PAIR)],
             send_sem=d_send.at[n], recv_sem=d_recv.at[n],
             device_id=(grp, to_seq, target), device_id_type=MESH,
         )
@@ -493,12 +493,12 @@
 
     @pl.when(seq < N_SEQ // 2)
     def _():
-        dec_ref[:, pl.ds(pl.multiple_of(smp * cols, HD), cols)] = dsend[smp]
+        dec_ref[:, :, pl.ds(pl.multiple_of(smp * cols, HD), cols)] = dsend[smp]
 
     @pl.when(seq >= N_SEQ // 2)
     def _():
         col = pl.multiple_of((1 - side) * shared * HD + (shared - 2) * HD, HD)
-        dec_ref[:, pl.ds(pl.multiple_of(smp * cols + col, HD), PAIR)] = dsend[smp, :, pl.ds(col, PAIR)]
+        dec_ref[:, :, pl.ds(pl.multiple_of(smp * cols + col, HD), PAIR)] = dsend[smp, :, :, pl.ds(col, PAIR)]
 
     for kind, size in ((I1, half), (J1, half), (I2, quarter), (J2, quarter), (Y, 3 * half)):
         ref = w.at[:, pl.ds(0, size)]
@@ -511,7 +511,7 @@
     kv_wait(2, 3)
     pltpu.make_async_copy(obuf, obuf, o_sem).wait()
 
-    early = dsend.at[:, :, pl.ds(0, cols - PAIR)]
+    early = dsend.at[:, :, :, pl.ds(0, cols - PAIR)]
 
     @pl.when(seq < N_SEQ // 2)
     def _():
@@ -522,12 +522,26 @@
 
     @pl.when(seq >= N_SEQ // 2)
     def _():
-        part = dsend.at[pl.ds(0, N_SMP - 1), :, pl.ds(0, PAIR)]
+        part = dsend.at[pl.ds(0, N_SMP - 1), :, :, pl.ds(0, PAIR)]
         pltpu.make_async_copy(part, part, d_send.at[0]).wait()
         pltpu.make_async_copy(early, early, d_recv.at[1]).wait()
         pltpu.make_async_copy(part, part, d_recv.at[0]).wait()
 
     dout_ref[...] = dec_ref[...].astype(jnp.bfloat16)
+
+
+def deliver(p_ref, d_ref, out_ref, dec_ref, p_buf, d_buf, sem):
+    size = p_ref.shape[0] // OUT_CUTS
+    ways = [(d_ref, d_buf, dec_ref)]
+    for n in range(OUT_CUTS):
+        ways.append(tuple(ref.at[pl.ds(n * size, size)] for ref in (p_ref, p_buf, out_ref)))
+    for n, (src, buf, _) in enumerate(ways):
+        pltpu.make_async_copy(src, buf, sem.at[0, n]).start()
+    for n, (src, buf, dst) in enumerate(ways):
+        pltpu.make_async_copy(src, buf, sem.at[0, n]).wait()
+        pltpu.make_async_copy(buf, dst, sem.at[1, n]).start()
+    for n, (_, buf, dst) in enumerate(ways):
+        pltpu.make_async_copy(buf, dst, sem.at[1, n]).wait()
 
 
 def local(prompt_x, sampled_x, w_query, w_key, w_value, q_gain, k_gain):
@@ -539,7 +553,7 @@
     shared = heads // 2
     chunks = SUBS * (1 + shared // 2)
     count = rows + drows
-    mine = drows // N_SMP
+    own = samples // N_SMP
     hbm = pl.BlockSpec(memory_space=pltpu.HBM)
     vmem = pl.BlockSpec(memory_space=pltpu.VMEM)
     dma = pltpu.SemaphoreType.DMA
@@ -547,7 +561,7 @@
         kernel,
         out_shape=(
             jax.ShapeDtypeStruct((rows, q_cols), jnp.bfloat16),
-            jax.ShapeDtypeStruct((mine, N_SMP * q_cols), jnp.bfloat16),
+            jax.ShapeDtypeStruct((own, steps, N_SMP * q_cols), jnp.bfloat16),
         ),
         in_specs=[hbm] * 7,
         out_specs=(pl.BlockSpec(memory_space=pl.ANY), vmem),
@@ -566,8 +580,8 @@
             pltpu.VMEM((2, drows, PAIR), jnp.bfloat16),
             pltpu.VMEM((heads, count, HD), jnp.bfloat16),
             pltpu.VMEM((heads, rows, HD), jnp.bfloat16),
-            pltpu.VMEM((N_SMP, mine, q_cols), jnp.float32),
-            pltpu.VMEM((mine, N_SMP * q_cols), jnp.float32),
+            pltpu.VMEM((N_SMP, own, steps, q_cols), jnp.float32),
+            pltpu.VMEM((own, steps, N_SMP * q_cols), jnp.float32),
             dma((2,)),
             dma((3,)),
             dma,
@@ -586,7 +600,21 @@
             collective_id=0, has_side_effects=True, vmem_limit_bytes=58 * 2**20
         ),
     )(prompt_x, sampled_x, w_query, w_key, w_value, q_gain.reshape(1, HD), k_gain.reshape(1, HD))
-    return prefill, dec.reshape(samples // N_SMP, steps, N_SMP * q_cols)
+    return pl.pallas_call(
+        deliver,
+        out_shape=(
+            jax.ShapeDtypeStruct((rows, q_cols), jnp.bfloat16),
+            jax.ShapeDtypeStruct((own, steps, N_SMP * q_cols), jnp.bfloat16),
+        ),
+        in_specs=[hbm, hbm],
+        out_specs=(hbm, hbm),
+        scratch_shapes=[
+            pltpu.VMEM((rows, q_cols), jnp.bfloat16),
+            pltpu.VMEM((own, steps, N_SMP * q_cols), jnp.bfloat16),
+            dma((2, 1 + OUT_CUTS)),
+        ],
+        compiler_params=pltpu.CompilerParams(vmem_limit_bytes=58 * 2**20),
+    )(prefill, dec)
 
 
 def solution(mesh):

time: 103 us -> 99.6 us (0.967)
  local copies, waits for them, and re-layouts: 3.88 us -> 0 us
    unnamed x1 -> x0, local copies, waits for them, and re-layouts: 2.26 us -> none
    pallas_call x0 -> x1, Pallas kernels: none -> 2.07 us  [local(): pl.pallas_call(deliver, out_shape=(jax.ShapeDtypeStruct((rows, q_cols), j...]
    pallas_call x1, Pallas kernels: 98.4 us -> 96.8 us  [local(): pl.pallas_call(kernel, out_shape=(jax.ShapeDtypeStruct((rows, q_cols), jn...]
    reshape x1 -> x0, local copies, waits for them, and re-layouts: 1.62 us -> none  [local(): return (prefill, dec.reshape(samples // N_SMP, steps, N_SMP * q_cols))]
where the time goes in v3:
time: 99.6 us; the launch traced here: 99.5 us
  Pallas kernels  98.8 us (99%)
    pallas_call x1, Pallas kernels, local(): pl.pallas_call(kernel, out_shape=(jax.ShapeDtypeStruct((rows, q_cols), jn...  96.8 us
    pallas_call x1, Pallas kernels, local(): pl.pallas_call(deliver, out_shape=(jax.ShapeDtypeStruct((rows, q_cols), j...  2.07 us

profile of v3, /device:TPU:1, one launch (start us, length us, event | category | flops | bytes accessed | tf_op | source)
XLA Modules:
  0.0 99.5 jit_solution(14684862657758444911)
XLA Ops:
  0.6 96.8 %shard_map.86 = (bf16[512,1024]{1,0:T(8,128)(2,1)}, bf16[2,4,8192]{2,1,0:T(4,128)(2,1)}) custom-call(bf16[512,5120]{1,0:T(8,128)(2,1)} %px_ref.1, bf16[16,4,5120]{2,1,0:T(4,128)(2,1)} %sx_ref.1, bf16[1280,1024]{1,0:T(8,128)(2,1)} %wq_ref.1, bf16[1280,128]{1,0:T(8,128)(2,1)} %wk_ref.1, bf16[1280,128]{1,0:T(8,128)(2,1)} %wv_ref.1, f32[1,128]{1,0:T(1,128)} %bitcast.2, ...), custom_call_target="tpu_custom_call" | custom-call | tf_op jit(solution)/shard_map/pallas_call | solution.py:560
  97.4 2.1 %shard_map.87 = (bf16[512,1024]{1,0:T(8,128)(2,1)}, bf16[2,4,8192]{2,1,0:T(4,128)(2,1)}) custom-call(bf16[512,1024]{1,0:T(8,128)(2,1)} %get-tuple-element.4.p_ref, bf16[2,4,8192]{2,1,0:T(4,128)(2,1)} %get-tuple-element.5.d_ref), custom_call_target="tpu_custom_call" | custom-call | tf_op jit(solution)/shard_map/pallas_call | solution.py:603

commit v4 on v3

--- a/solution.py
+++ b/solution.py
@@ -72,7 +72,8 @@
     up = lax.rem(seq + 1, N_SEQ)
     down = lax.rem(seq + N_SEQ - 1, N_SEQ)
     far = lax.rem(seq + 2, N_SEQ)
-    mirror = N_SEQ - 1 - seq
+    mirror = seq + 1 - 2 * lax.rem(seq, 2)
+    decodes = (seq == 1) | (seq == 2)
     near = lax.rem(seq + 2 * lo + N_SEQ - 1, N_SEQ)
     other = lax.rem(seq + N_SEQ + 1 - 2 * lo, N_SEQ)
     lo_grp = (1 - lo) * N_Y + y
@@ -239,7 +240,7 @@
         cosine = jnp.cos(angle)
         sine = jnp.sin(angle)
         sine = jnp.where(lane < HD // 2, -sine, sine)
-        fold = HD ** (-0.5) * math.log2(math.e)
+        fold = HD ** (-0.5)
         for n, factor in enumerate((1.0, fold)):
             gain = gains[n] * factor
             tabs[n, 0] = cosine * gain
@@ -276,17 +277,17 @@
     def attend_blocks(h, full):
         for r in range(2):
             q = qbuf[h, pl.ds(r * tile, tile)]
-            e = jnp.exp2(dot_t(q, kvx[full, 0, pl.ds(r * tile, tile)]))
+            e = jnp.exp(dot_t(q, kvx[full, 0, pl.ds(r * tile, tile)]))
             allowed = lax.broadcasted_iota(jnp.int32, (tile, tile), 1) <= lax.broadcasted_iota(
                 jnp.int32, (tile, tile), 0
             )
             e = jnp.where(allowed, e, 0.0).astype(jnp.bfloat16)
             total = dot(e, vaug[full, pl.ds(r * tile, tile)])
             if r > 0:
-                e = jnp.exp2(dot_t(q, kvx[full, 0, pl.ds(0, tile)])).astype(jnp.bfloat16)
+                e = jnp.exp(dot_t(q, kvx[full, 0, pl.ds(0, tile)])).astype(jnp.bfloat16)
                 total += dot(e, vaug[full, pl.ds(0, tile)])
             for j in range(full):
-                e = jnp.exp2(dot_t(q, kvx[j, 0])).astype(jnp.bfloat16)
+                e = jnp.exp(dot_t(q, kvx[j, 0])).astype(jnp.bfloat16)
                 total += dot(e, vaug[j])
             obuf[h, pl.ds(r * tile, tile)] = (total[:, :HD] / total[:, HD:]).astype(jnp.bfloat16)
 
@@ -294,10 +295,10 @@
         q = qbuf[h, pl.ds(rows, drows)]
         a = lax.broadcasted_iota(jnp.int32, (drows, drows), 0)
         b = lax.broadcasted_iota(jnp.int32, (drows, drows), 1)
-        own = jnp.where((b <= a) & (a // 4 == b // 4), jnp.exp2(dot_t(q, kvd[0, :, :HD])), 0.0)
+        own = jnp.where((b <= a) & (a // 4 == b // 4), jnp.exp(dot_t(q, kvd[0, :, :HD])), 0.0)
         total = dot(own.astype(jnp.bfloat16), kvd[1])
         for j in range(N_SEQ):
-            total += dot(jnp.exp2(dot_t(q, kvx[j, 0])).astype(jnp.bfloat16), vaug[j])
+            total += dot(jnp.exp(dot_t(q, kvx[j, 0])).astype(jnp.bfloat16), vaug[j])
         res = total[:, :HD] / total[:, HD:]
         dsend[:, :, :, pl.ds(pl.multiple_of(h * HD, HD), HD)] = res.reshape(dsend.shape[:3] + (HD,))
 
@@ -366,14 +367,14 @@
             q_message(j).wait_recv()
             q_message(j + 1).wait_recv()
 
-        @pl.when(opening & ((seq < N_SEQ // 2) | (g == shared - 1)))
+        @pl.when(opening & (decodes | (g == shared - 1)))
         def _():
             attend_samples(first)
             attend_samples(first + 1)
             for d in range(1, N_SMP):
                 d_message(g, 0, seq, lax.rem(smp + d, N_SMP)).start()
 
-        @pl.when(opening & (seq < N_SEQ // 2) & (g < shared - 1))
+        @pl.when(opening & decodes & (g < shared - 1))
         def _():
             for d in range(N_SMP):
                 d_message(g, 1, mirror, lax.rem(smp + d, N_SMP)).start()
@@ -491,11 +492,11 @@
 
     lax.fori_loop(0, chunks + LAG, step, 0)
 
-    @pl.when(seq < N_SEQ // 2)
+    @pl.when(decodes)
     def _():
         dec_ref[:, :, pl.ds(pl.multiple_of(smp * cols, HD), cols)] = dsend[smp]
 
-    @pl.when(seq >= N_SEQ // 2)
+    @pl.when(jnp.logical_not(decodes))
     def _():
         col = pl.multiple_of((1 - side) * shared * HD + (shared - 2) * HD, HD)
         dec_ref[:, :, pl.ds(pl.multiple_of(smp * cols + col, HD), PAIR)] = dsend[smp, :, :, pl.ds(col, PAIR)]
@@ -513,14 +514,14 @@
 
     early = dsend.at[:, :, :, pl.ds(0, cols - PAIR)]
 
-    @pl.when(seq < N_SEQ // 2)
+    @pl.when(decodes)
     def _():
         part = dsend.at[pl.ds(0, N_SMP - 1)]
         pltpu.make_async_copy(early, early, d_send.at[1]).wait()
         pltpu.make_async_copy(part, part, d_send.at[0]).wait()
         pltpu.make_async_copy(part, part, d_recv.at[0]).wait()
 
-    @pl.when(seq >= N_SEQ // 2)
+    @pl.when(jnp.logical_not(decodes))
     def _():
         part = dsend.at[pl.ds(0, N_SMP - 1), :, :, pl.ds(0, PAIR)]
         pltpu.make_async_copy(part, part, d_send.at[0]).wait()

time: 99.6 us -> 99.7 us (level)
  no operation moved by 1% of the time
where the time goes in v4:
time: 99.7 us; the launch traced here: 99.6 us
  Pallas kernels  99 us (99%)
    pallas_call x1, Pallas kernels, local(): pl.pallas_call(kernel, out_shape=(jax.ShapeDtypeStruct((rows, q_cols), jn...  96.9 us
    pallas_call x1, Pallas kernels, local(): pl.pallas_call(deliver, out_shape=(jax.ShapeDtypeStruct((rows, q_cols), j...  2.07 us

profile of v4, /device:TPU:1, one launch (start us, length us, event | category | flops | bytes accessed | tf_op | source)
XLA Modules:
  0.0 99.6 jit_solution(4336466173808713954)
XLA Ops:
  0.6 96.9 %shard_map.86 = (bf16[512,1024]{1,0:T(8,128)(2,1)}, bf16[2,4,8192]{2,1,0:T(4,128)(2,1)}) custom-call(bf16[512,5120]{1,0:T(8,128)(2,1)} %px_ref.1, bf16[16,4,5120]{2,1,0:T(4,128)(2,1)} %sx_ref.1, bf16[1280,1024]{1,0:T(8,128)(2,1)} %wq_ref.1, bf16[1280,128]{1,0:T(8,128)(2,1)} %wk_ref.1, bf16[1280,128]{1,0:T(8,128)(2,1)} %wv_ref.1, f32[1,128]{1,0:T(1,128)} %bitcast.2, ...), custom_call_target="tpu_custom_call" | custom-call | tf_op jit(solution)/shard_map/pallas_call | solution.py:561
  97.5 2.1 %shard_map.87 = (bf16[512,1024]{1,0:T(8,128)(2,1)}, bf16[2,4,8192]{2,1,0:T(4,128)(2,1)}) custom-call(bf16[512,1024]{1,0:T(8,128)(2,1)} %get-tuple-element.4.p_ref, bf16[2,4,8192]{2,1,0:T(4,128)(2,1)} %get-tuple-element.5.d_ref), custom_call_target="tpu_custom_call" | custom-call | tf_op jit(solution)/shard_map/pallas_call | solution.py:604

commit v5 on v4

--- a/solution.py
+++ b/solution.py
@@ -22,8 +22,9 @@
 AT_I2 = 2
 AT_J2 = 3
 LAG = 5
-KV_ON = 12
-KV_END = 14
+KV_AT = (12, 13)
+KV_ON = 16
+KV_END = 18
 X_START = (3, 5, 7, 9)
 X_STEPS = (11, 15, 19, 23, 16, 20, 24, 27, 28, 30)
 PARTNER_AT = (15, 15, 16, 16, 16, 17, 17, 18, 18, 19)
@@ -473,14 +474,17 @@
                 kvx[seq, 1] = v[:rows]
                 kvd[0, :, :HD] = k[rows:]
                 kvd[1, :, :HD] = v[rows:]
-                for part in range(2):
-                    for way in range(2):
-                        kv_own(part, way).start()
 
             @pl.when((t >= SUBS) & (lax.rem(t, SUBS) == SUBS - 1))
             def _():
                 for k in range(2):
                     qbuf[side * shared + (t // SUBS - 1) * 2 + k] = rotated(1, proj[1, :, k * HD : (k + 1) * HD])
+
+        for part, at in enumerate(KV_AT):
+            @pl.when(i == at)
+            def _(part=part):
+                for way in range(2):
+                    kv_own(part, way).start()
 
         @pl.when(i == KV_END)
         def _():

time: 99.7 us -> 98.1 us (0.984)
  Pallas kernels: 99 us -> 97 us
    pallas_call x1, Pallas kernels: 96.9 us -> 94.9 us  [local(): pl.pallas_call(kernel, out_shape=(jax.ShapeDtypeStruct((rows, q_cols), jn...]
where the time goes in v5:
time: 98.1 us; the launch traced here: 97.6 us
  Pallas kernels  97 us (99%)
    pallas_call x1, Pallas kernels, local(): pl.pallas_call(kernel, out_shape=(jax.ShapeDtypeStruct((rows, q_cols), jn...  94.9 us
    pallas_call x1, Pallas kernels, local(): pl.pallas_call(deliver, out_shape=(jax.ShapeDtypeStruct((rows, q_cols), j...  2.07 us

profile of v5, /device:TPU:1, one launch (start us, length us, event | category | flops | bytes accessed | tf_op | source)
XLA Modules:
  0.0 97.6 jit_solution(14771610663848323082)
XLA Ops:
  0.6 94.9 %shard_map.86 = (bf16[512,1024]{1,0:T(8,128)(2,1)}, bf16[2,4,8192]{2,1,0:T(4,128)(2,1)}) custom-call(bf16[512,5120]{1,0:T(8,128)(2,1)} %px_ref.1, bf16[16,4,5120]{2,1,0:T(4,128)(2,1)} %sx_ref.1, bf16[1280,1024]{1,0:T(8,128)(2,1)} %wq_ref.1, bf16[1280,128]{1,0:T(8,128)(2,1)} %wk_ref.1, bf16[1280,128]{1,0:T(8,128)(2,1)} %wv_ref.1, f32[1,128]{1,0:T(1,128)} %bitcast.2, ...), custom_call_target="tpu_custom_call" | custom-call | tf_op jit(solution)/shard_map/pallas_call | solution.py:565
  95.5 2.1 %shard_map.87 = (bf16[512,1024]{1,0:T(8,128)(2,1)}, bf16[2,4,8192]{2,1,0:T(4,128)(2,1)}) custom-call(bf16[512,1024]{1,0:T(8,128)(2,1)} %get-tuple-element.4.p_ref, bf16[2,4,8192]{2,1,0:T(4,128)(2,1)} %get-tuple-element.5.d_ref), custom_call_target="tpu_custom_call" | custom-call | tf_op jit(solution)/shard_map/pallas_call | solution.py:608
